TPU v7x, 256 devices: a whole 4x4x8 slice. The times are simulated.
256 devices in a mesh: example: 64 (over x, z, core), feature: 4 (over y).
Axes of the slice: x: 4, y: 4, z: 8, core: 2. Of those that a mesh axis runs over, the one named last changes fastest.
Arguments:
- embeddings: bfloat16 [36864, 16384], P('example', 'feature'), may hold values from -16 to 16
- subspace: bfloat16 [16384, 128], P('feature'), may hold values from -0.046875 to 0.046875
- noise_levels: int32 [16384, 128], P('feature'), may hold values from -16 to 16
- targets: int32 [2048], replicated, may hold values from 0 to 16383
Outputs:
- embedding_grad: bfloat16 [36864, 16384], P('example', 'feature')
All inputs are finite; a program needn't handle non-finite values.
Results may differ from a plain program's by a relative error of at most 0.0085.
Values may be sent and summed in bfloat16 or wider, within the bound.
A program may use at most 64 MiB of HBM per device.

v0:
```python
import jax
import jax.numpy as jnp
from jax import lax
from jax.sharding import PartitionSpec as P

NOISE_STEP = 1.0 / 4096.0
HIGH = lax.Precision.HIGHEST


def transposed(former, latter, precision=None):
    return lax.dot_general(
        former,
        latter,
        (((0,), (0,)), ((), ())),
        precision=precision,
        preferred_element_type=jnp.float32,
    )


def by_columns(former, latter):
    return lax.dot_general(
        former, latter, (((1,), (1,)), ((), ())), preferred_element_type=jnp.float32
    )


def count_rows(targets, first, length):
    local = targets - first
    inside = (local >= 0) & (local < length)
    slots = jnp.where(inside, local, length)
    ones = jnp.ones(targets.shape, jnp.float32)
    return jax.ops.segment_sum(ones, slots, num_segments=length + 1)[:length]


def upper_factor(gram_matrix):
    return jnp.linalg.cholesky(gram_matrix).T


def factorize(gram_matrix):
    lower_factor = jnp.linalg.cholesky(gram_matrix)
    identity = jnp.eye(gram_matrix.shape[0], dtype=jnp.float32)
    inverse_factor = jax.scipy.linalg.solve_triangular(lower_factor, identity, lower=True)
    gram_inverse = jnp.dot(inverse_factor.T, inverse_factor, precision=HIGH)
    return (inverse_factor, gram_inverse)


def on_device(embeddings, subspace, noise_levels, targets):
    row_count, local_width = embeddings.shape
    examples = lax.axis_size("example")
    total_rows = row_count * examples
    projected = lax.psum(
        jnp.dot(embeddings, subspace, preferred_element_type=jnp.float32), "feature"
    )
    projected_low = projected.astype(jnp.bfloat16)
    feature_first = lax.axis_index("feature") * local_width
    share = local_width // examples
    summed = lax.psum_scatter(
        transposed(embeddings, projected_low), "example", scatter_dimension=0, tiled=True
    )
    offset = lax.axis_index("example") * share
    noise_part = lax.dynamic_slice_in_dim(noise_levels, offset, share, 0)
    image = summed / total_rows + NOISE_STEP * noise_part.astype(jnp.float32)
    row_counts = count_rows(targets, feature_first + offset, share)
    gram_matrix = lax.psum(transposed(image, image, HIGH), ("example", "feature"))
    inverse_factor, gram_inverse = factorize(gram_matrix)
    orthonormal = jnp.dot(image, inverse_factor.T, precision=HIGH)
    alignment = lax.psum(
        transposed(orthonormal * row_counts[:, None], orthonormal, HIGH), ("example", "feature")
    )
    factor_grad = 2.0 * jnp.dot(alignment, inverse_factor, precision=HIGH)
    unused, pull_back = jax.vjp(upper_factor, gram_matrix)
    gram_grad = pull_back(factor_grad)[0]
    image_grad = jnp.dot(image, gram_grad + gram_grad.T, precision=HIGH) - 2.0 * row_counts[
        :, None
    ] * jnp.dot(image, gram_inverse, precision=HIGH)
    grad_low = image_grad.astype(jnp.bfloat16)
    grad_low = lax.all_gather(grad_low, "example", axis=0, tiled=True)
    back_sum = lax.psum(
        jnp.dot(embeddings, grad_low, preferred_element_type=jnp.float32), "feature"
    )
    back_rows = back_sum.astype(jnp.bfloat16)
    result = by_columns(projected_low, grad_low) + by_columns(back_rows, subspace)
    return result.astype(jnp.bfloat16)


def solution(mesh):
    in_specs = (P("example", "feature"), P("feature", None), P("feature", None), P())
    out_specs = P("example", "feature")
    return jax.shard_map(
        on_device, mesh=mesh, in_specs=in_specs, out_specs=out_specs, check_vma=False
    )
```

profile of v0, /device:TPU:2, one launch (start us, length us, event | category | flops | bytes accessed | tf_op | source)
XLA Modules:
  0.0 797.7 jit_solution(3288870860719686440)
XLA Ops:
  6.5 0.0 copy-start
  6.5 0.0 reduce-scatter.4.cloned.1.call-start
  6.5 4.2 fusion.45
  10.7 20.2 %all-reduce.8 = bf16[576,128]{1,0:T(8,128)(2,1)S(1)} all-reduce(f32[576,128]{1,0:T(8,128)S(1)} %fusion.45), channel_id=1, replica_groups=mesh['example'=64,'feature'=4] {'feature'}, use_global_device_ids=true, to_apply=%region_0.0 | all-reduce | flops 73728 | bytes 442368 | tf_op jit(solution)/shard_map/psum | solution.py:50
  30.9 4.7 convolution_bitcast_fusion
  35.6 0.0 copy-start.3
  35.6 2.9 copy.14
  38.5 0.0 reduce-scatter.4.cloned.1.call-update
  38.6 0.0 all-reduce.5.cloned.1.call-start
  38.6 0.0 copy-done
  38.6 0.1 copy.16
  38.7 0.0 copy-done.3
  38.8 14.7 %scatter_custom_fusion = f32[65]{0:T(128)S(1)} fusion(s32[2048]{0:T(1024)S(1)} %and_select_fusion, f32[2048]{0:T(1024)S(1)} %broadcast.95, f32[]{:T(128)} %constant.76.clone.1), kind=kCustom, calls=%fused_computation.59 | custom fusion | flops 2048 | bytes 264 | tf_op jit(solution)/shard_map/scatter-add | solution.py:31
  53.5 126.3 %reduce-scatter.4.cloned.1.call-done = f32[64,128]{1,0:T(8,128)} async-done(((f32[4096,128]{1,0:T(8,128)}), f32[64,128]{1,0:T(8,128)}) %reduce-scatter.4.cloned.1.call-update) | async-done | bytes 32784
  179.7 0.8 copy.15
  180.6 0.9 fusion.46
  181.5 0.0 all-reduce.5.cloned.1.call-update
  181.5 0.0 all-reduce.7.cloned.1.call-start
  181.6 240.4 %all-reduce.5.cloned.1.call-done = f32[128,128]{0,1:T(8,128)} async-done(((f32[128,128]{0,1:T(8,128)}), f32[128,128]{0,1:T(8,128)}) %all-reduce.5.cloned.1.call-update) | async-done | bytes 65552 | tf_op jit(solution)/shard_map/psum | solution.py:63
  422.0 0.9 copy.11
  423.0 0.9 fusion.22
  423.8 11.7 %custom-call.14 = f32[128,128]{1,0:T(8,128)S(1)} custom-call(f32[128,128]{1,0:T(8,128)S(1)} %fusion.22), custom_call_target="Cholesky" | custom-call | tf_op jit(solution)/shard_map/jvp(jit(cholesky))/cholesky/custom-call.1 | solution.py:35
  435.6 0.7 compare_reduce_fusion
  436.2 0.6 fusion.24
  436.9 9.8 %custom-call.13 = f32[1,128,128]{1,2,0:T(8,128)S(1)} custom-call(f32[1,128,128]{2,1,0:T(8,128)S(1)} %fusion.24), custom_call_target="InvertDiagBlocksLowerTriangular" | custom-call | tf_op jit(solution)/shard_map/transpose(jvp(jit(cholesky)))/triangular_solve | solution.py:35
  446.7 0.2 fusion.20
  446.9 0.3 fusion.47
  447.2 1.0 fusion.29
  448.2 0.0 all-reduce.7.cloned.1.call-update
  448.2 0.2 all-gather.2.cloned.1.call-start
  448.5 0.3 fusion.48
  448.7 233.9 %all-reduce.7.cloned.1.call-done = f32[128,128]{1,0:T(8,128)} async-done(((f32[128,128]{1,0:T(8,128)}), f32[128,128]{1,0:T(8,128)}) %all-reduce.7.cloned.1.call-update) | async-done | bytes 65552 | tf_op jit(solution)/shard_map/psum | solution.py:66
  682.6 1.1 fusion.1
  683.7 0.9 fusion
  684.6 0.2 fusion.18
  684.9 0.3 fusion.16
  685.1 0.1 copy.12
  685.2 0.3 fusion.12
  685.5 0.9 fusion.3
  686.4 0.0 all-gather.2.cloned.1.call-update
  686.4 72.9 %all-gather.2.cloned.1.call-done = bf16[4096,128]{1,0:T(8,128)(2,1)} async-done(((bf16[64,128]{1,0:T(8,128)(2,1)}), bf16[4096,128]{1,0:T(8,128)(2,1)}) %all-gather.2.cloned.1.call-update) | async-done | bytes 1048592 | tf_op jit(solution)/shard_map/all_gather | solution.py:76
  759.3 5.2 convolution_bitcast_fusion.1
  764.5 21.6 %all-reduce.9 = bf16[576,128]{0,1:T(8,128)(2,1)S(1)} all-reduce(f32[576,128]{0,1:T(8,128)} %convolution_bitcast_fusion.1), channel_id=1, replica_groups=mesh['example'=64,'feature'=4] {'feature'}, use_global_device_ids=true, to_apply=%region_7.9 | all-reduce | flops 73728 | bytes 442368 | tf_op jit(solution)/shard_map/psum | solution.py:77
  786.1 0.0 copy-done.1
  786.1 0.0 copy-start.2
  786.1 1.4 fusion.49
  787.5 0.0 copy-done.2
  787.5 3.6 add_convert_fusion
  (8 shorter events, 0.1 us)
Async XLA Ops:
  6.5 32.1 %copy-start = (s32[4096,128]{1,0:T(8,128)S(1)}, s32[4096,128]{1,0:T(8,128)}, u32[]{:S(2)}) copy-start(s32[4096,128]{1,0:T(8,128)} %param.7) | copy-start | bytes 6291460
  6.5 173.2 %reduce-scatter.4.cloned.1.call-start = ((), (), s32[]{:S(2)}) async-start(), calls=%async_computation.4 | async-start | bytes 2129920
  35.6 3.2 copy-start.3
  38.6 383.5 %all-reduce.5.cloned.1.call-start = ((), (), s32[]{:S(2)}) async-start(), calls=%async_computation.1 | async-start | bytes 131072 | tf_op jit(solution)/shard_map/psum | solution.py:63
  181.5 501.1 %all-reduce.7.cloned.1.call-start = ((), (), s32[]{:S(2)}) async-start(), calls=%async_computation.2 | async-start | bytes 131072 | tf_op jit(solution)/shard_map/psum | solution.py:66
  448.2 311.1 %all-gather.2.cloned.1.call-start = ((), (), s32[]{:S(2)}) async-start(), calls=%async_computation.3 | async-start | bytes 1064960 | tf_op jit(solution)/shard_map/all_gather | solution.py:76
  759.3 26.8 %copy-start.1 = (bf16[4096,128]{1,0:T(8,128)(2,1)S(1)}, bf16[4096,128]{1,0:T(8,128)(2,1)}, u32[]{:S(2)}) copy-start(bf16[4096,128]{1,0:T(8,128)(2,1)} %all-gather.2.cloned.1.call-done) | copy-start | bytes 3145732
  786.1 1.4 copy-start.2
Sparse Core Ops, SparseCore 0:
  38.7 140.9 reduce-scatter.3
  186.1 235.8 all-reduce.4
  448.3 234.2 all-reduce.6
  686.6 72.6 all-gather.1
where the time goes:
time: 798 us
  waiting for transfers between devices  674 us (84%)
  blocking collectives  41.8 us (5%)
  other arithmetic  38.4 us (5%)
  matrix products  25.4 us (3%)
  between operations  13.3 us (2%)
    psum x1, waiting for transfers between devices, on_device(): lax.psum(transposed(image, image, HIGH), ('example', 'feature'))  240 us
    psum x1, waiting for transfers between devices, on_device(): lax.psum(transposed(orthonormal * row_counts[:, None], orthonormal, HIGH)...  234 us
    unnamed x5, waiting for transfers between devices  126 us
    all_gather x1, waiting for transfers between devices, on_device(): grad_low = lax.all_gather(grad_low, 'example', axis=0, tiled=True)  72.9 us
    another operation x5, other arithmetic, upper_factor(): return jnp.linalg.cholesky(gram_matrix).T  22.8 us
    psum x1, blocking collectives, on_device(): lax.psum(jnp.dot(embeddings, grad_low, preferred_element_type=jnp.float32...  21.6 us
    psum x1, blocking collectives, on_device(): lax.psum(jnp.dot(embeddings, subspace, preferred_element_type=jnp.float32...  20.2 us
  transfers between devices with their start and end apart: 4, of which 4 were waited for; matrix products, arithmetic and copies ran while one was open for 2% of the time, Pallas kernels for 0%

commit v1 on v0

--- a/solution.py
+++ b/solution.py
@@ -64,7 +64,8 @@
     inverse_factor, gram_inverse = factorize(gram_matrix)
     orthonormal = jnp.dot(image, inverse_factor.T, precision=HIGH)
     alignment = lax.psum(
-        transposed(orthonormal * row_counts[:, None], orthonormal, HIGH), ("example", "feature")
+        lax.psum(transposed(orthonormal * row_counts[:, None], orthonormal, HIGH), "feature"),
+        "example",
     )
     factor_grad = 2.0 * jnp.dot(alignment, inverse_factor, precision=HIGH)
     unused, pull_back = jax.vjp(upper_factor, gram_matrix)

time: 798 us -> 778 us (0.975)
  waiting for transfers between devices: 674 us -> 654 us
    psum x1, waiting for transfers between devices: 234 us -> 43.3 us  [on_device(): lax.psum(transposed(orthonormal * row_counts[:, None], orthonormal, HIGH)...]
    psum x0 -> x1, waiting for transfers between devices: none -> 171 us  [on_device(): lax.psum(lax.psum(transposed(orthonormal * row_counts[:, None], orthonorm...]
    unnamed x5 -> x6, waiting for transfers between devices: 126 us -> 126 us
  transfers between devices with their start and end apart: 4 -> 5, of which waited for: 4 -> 5; matrix products, arithmetic and copies ran while one was open for 2% -> 2% of each run, Pallas kernels for 0% -> 0%
where the time goes in v1:
time: 778 us
  waiting for transfers between devices  654 us (84%)
  blocking collectives  41.8 us (5%)
  other arithmetic  38.3 us (5%)
  matrix products  25.4 us (3%)
  between operations  13.4 us (2%)
    psum x1, waiting for transfers between devices, on_device(): lax.psum(transposed(image, image, HIGH), ('example', 'feature'))  240 us
    psum x1, waiting for transfers between devices, on_device(): lax.psum(lax.psum(transposed(orthonormal * row_counts[:, None], orthonorm...  171 us
    unnamed x6, waiting for transfers between devices  126 us
    all_gather x1, waiting for transfers between devices, on_device(): grad_low = lax.all_gather(grad_low, 'example', axis=0, tiled=True)  73.3 us
    psum x1, waiting for transfers between devices, on_device(): lax.psum(transposed(orthonormal * row_counts[:, None], orthonormal, HIGH)...  43.3 us
    another operation x5, other arithmetic, upper_factor(): return jnp.linalg.cholesky(gram_matrix).T  22.8 us
    psum x1, blocking collectives, on_device(): lax.psum(jnp.dot(embeddings, grad_low, preferred_element_type=jnp.float32...  21.6 us
    psum x1, blocking collectives, on_device(): lax.psum(jnp.dot(embeddings, subspace, preferred_element_type=jnp.float32...  20.2 us
  transfers between devices with their start and end apart: 5, of which 5 were waited for; matrix products, arithmetic and copies ran while one was open for 2% of the time, Pallas kernels for 0%

profile of v1, /device:TPU:2, one launch (start us, length us, event | category | flops | bytes accessed | tf_op | source)
XLA Modules:
  0.0 778.0 jit_solution(15669929040957145166)
XLA Ops:
  6.5 0.0 copy-start
  6.5 0.0 reduce-scatter.4.cloned.1.call-start
  6.5 4.2 fusion.45
  10.7 20.2 %all-reduce.11 = bf16[576,128]{1,0:T(8,128)(2,1)S(1)} all-reduce(f32[576,128]{1,0:T(8,128)S(1)} %fusion.45), channel_id=1, replica_groups=mesh['example'=64,'feature'=4] {'feature'}, use_global_device_ids=true, to_apply=%region_0.0 | all-reduce | flops 73728 | bytes 442368 | tf_op jit(solution)/shard_map/psum | solution.py:50
  30.9 4.7 convolution_bitcast_fusion
  35.6 2.9 copy.14
  38.5 0.0 reduce-scatter.4.cloned.1.call-update
  38.6 0.0 all-reduce.6.cloned.1.call-start
  38.6 0.0 copy-done
  38.6 0.1 copy.16
  38.7 0.0 copy-done.3
  38.8 14.7 %scatter_custom_fusion = f32[65]{0:T(128)S(1)} fusion(s32[2048]{0:T(1024)S(1)} %and_select_fusion, f32[2048]{0:T(1024)S(1)} %broadcast.95, f32[]{:T(128)} %constant.76.clone.1), kind=kCustom, calls=%fused_computation.59 | custom fusion | flops 2048 | bytes 264 | tf_op jit(solution)/shard_map/scatter-add | solution.py:31
  53.4 126.3 %reduce-scatter.4.cloned.1.call-done = f32[64,128]{1,0:T(8,128)} async-done(((f32[4096,128]{1,0:T(8,128)}), f32[64,128]{1,0:T(8,128)}) %reduce-scatter.4.cloned.1.call-update) | async-done | bytes 32784
  179.7 0.8 copy.15
  180.6 0.9 fusion.46
  181.5 0.0 all-reduce.6.cloned.1.call-update
  181.5 0.0 all-reduce.8.cloned.1.call-start
  181.6 240.4 %all-reduce.6.cloned.1.call-done = f32[128,128]{0,1:T(8,128)} async-done(((f32[128,128]{0,1:T(8,128)}), f32[128,128]{0,1:T(8,128)}) %all-reduce.6.cloned.1.call-update) | async-done | bytes 65552 | tf_op jit(solution)/shard_map/psum | solution.py:63
  422.0 0.9 copy.11
  423.0 0.9 fusion.22
  423.8 11.7 %custom-call.14 = f32[128,128]{1,0:T(8,128)S(1)} custom-call(f32[128,128]{1,0:T(8,128)S(1)} %fusion.22), custom_call_target="Cholesky" | custom-call | tf_op jit(solution)/shard_map/jvp(jit(cholesky))/cholesky/custom-call.1 | solution.py:35
  435.6 0.6 compare_reduce_fusion
  436.2 0.6 fusion.24
  436.8 9.8 %custom-call.13 = f32[1,128,128]{1,2,0:T(8,128)S(1)} custom-call(f32[1,128,128]{2,1,0:T(8,128)S(1)} %fusion.24), custom_call_target="InvertDiagBlocksLowerTriangular" | custom-call | tf_op jit(solution)/shard_map/transpose(jvp(jit(cholesky)))/triangular_solve | solution.py:35
  446.6 0.2 fusion.20
  446.8 0.3 fusion.47
  447.1 1.0 fusion.29
  448.1 0.0 all-reduce.8.cloned.1.call-update
  448.1 0.0 all-reduce.10.cloned.1.call-start
  448.2 43.3 %all-reduce.8.cloned.1.call-done = f32[128,128]{1,0:T(8,128)} async-done(((f32[128,128]{1,0:T(8,128)}), f32[128,128]{1,0:T(8,128)}) %all-reduce.8.cloned.1.call-update) | async-done | bytes 65552 | tf_op jit(solution)/shard_map/psum | solution.py:67
  491.5 0.0 all-reduce.10.cloned.1.call-update
  491.5 0.2 all-gather.2.cloned.1.call-start
  491.7 0.3 fusion.48
  492.0 170.6 %all-reduce.10.cloned.1.call-done = f32[128,128]{1,0:T(8,128)} async-done(((f32[128,128]{1,0:T(8,128)}), f32[128,128]{1,0:T(8,128)}) %all-reduce.10.cloned.1.call-update) | async-done | bytes 65552 | tf_op jit(solution)/shard_map/psum | solution.py:66
  662.6 1.1 fusion.1
  663.7 0.8 fusion
  664.6 0.2 fusion.18
  664.8 0.3 fusion.16
  665.1 0.1 copy.12
  665.2 0.3 fusion.12
  665.5 0.9 fusion.3
  666.4 0.0 all-gather.2.cloned.1.call-update
  666.4 73.3 %all-gather.2.cloned.1.call-done = bf16[4096,128]{1,0:T(8,128)(2,1)} async-done(((bf16[64,128]{1,0:T(8,128)(2,1)}), bf16[4096,128]{1,0:T(8,128)(2,1)}) %all-gather.2.cloned.1.call-update) | async-done | bytes 1048592 | tf_op jit(solution)/shard_map/all_gather | solution.py:77
  739.7 5.2 convolution_bitcast_fusion.1
  744.9 21.6 %all-reduce.12 = bf16[576,128]{0,1:T(8,128)(2,1)S(1)} all-reduce(f32[576,128]{0,1:T(8,128)} %convolution_bitcast_fusion.1), channel_id=1, replica_groups=mesh['example'=64,'feature'=4] {'feature'}, use_global_device_ids=true, to_apply=%region_8.10 | all-reduce | flops 73728 | bytes 442368 | tf_op jit(solution)/shard_map/psum | solution.py:78
  766.5 0.0 copy-start.2
  766.5 1.4 fusion.49
  767.9 3.6 add_convert_fusion
  (11 shorter events, 0.1 us)
Async XLA Ops:
  6.5 32.1 %copy-start = (s32[4096,128]{1,0:T(8,128)S(1)}, s32[4096,128]{1,0:T(8,128)}, u32[]{:S(2)}) copy-start(s32[4096,128]{1,0:T(8,128)} %param.7) | copy-start | bytes 6291460
  6.5 173.2 %reduce-scatter.4.cloned.1.call-start = ((), (), s32[]{:S(2)}) async-start(), calls=%async_computation.5 | async-start | bytes 2129920
  35.6 3.2 copy-start.3
  38.6 383.5 %all-reduce.6.cloned.1.call-start = ((), (), s32[]{:S(2)}) async-start(), calls=%async_computation.1 | async-start | bytes 131072 | tf_op jit(solution)/shard_map/psum | solution.py:63
  181.5 309.9 %all-reduce.8.cloned.1.call-start = ((), (), s32[]{:S(2)}) async-start(), calls=%async_computation.2 | async-start | bytes 131072 | tf_op jit(solution)/shard_map/psum | solution.py:67
  448.1 214.5 %all-reduce.10.cloned.1.call-start = ((), (), s32[]{:S(2)}) async-start(), calls=%async_computation.3 | async-start | bytes 131072 | tf_op jit(solution)/shard_map/psum | solution.py:66
  491.5 248.2 %all-gather.2.cloned.1.call-start = ((), (), s32[]{:S(2)}) async-start(), calls=%async_computation.4 | async-start | bytes 1064960 | tf_op jit(solution)/shard_map/all_gather | solution.py:77
  739.7 26.8 %copy-start.1 = (bf16[4096,128]{1,0:T(8,128)(2,1)S(1)}, bf16[4096,128]{1,0:T(8,128)(2,1)}, u32[]{:S(2)}) copy-start(bf16[4096,128]{1,0:T(8,128)(2,1)} %all-gather.2.cloned.1.call-done) | copy-start | bytes 3145732
  766.5 1.4 copy-start.2
Sparse Core Ops, SparseCore 0:
  38.7 140.9 reduce-scatter.3
  186.1 235.8 all-reduce.5
  448.3 43.1 all-reduce.7
  494.8 167.7 all-reduce.9
  666.5 73.1 all-gather.1
